TPU v7x, 128 devices: a whole 4x4x4 slice. The times are simulated.
128 devices in a mesh: row: 8 (over z, y_lo), col: 16 (over x, y_hi, core).
Axes of the slice: x: 4, y: 4 (y_hi: 2, y_lo: 2; y = y_hi * 2 + y_lo), z: 4, core: 2. Of those that a mesh axis runs over, the one named last changes fastest.
Arguments:
- activations: bfloat16 [2048, 12288], P('col', 'row'), may hold values from -45 to 45
- qkv_weight: bfloat16 [12288, 3, 12288], P('row', None, 'col'), may hold values from -0.108253175 to 0.108253175
- out_weight: bfloat16 [12288, 12288], P('col', 'row'), may hold values from -0.21875 to 0.21875
Outputs:
- attn_out: bfloat16 [2048, 12288], P('col', 'row')
All inputs are finite; a program needn't handle non-finite values.
Results may differ from a plain program's by a relative error of at most 0.012.
The roundings to bfloat16 on the way count: a program that leaves them out, or rounds other values in their place, can miss the bound.
Values may be sent and summed in bfloat16 or wider, within the bound.
A program may use at most 128 MiB of HBM per device.

v0:
```python
import math

import jax
import jax.numpy as jnp
from jax import lax
from jax.sharding import PartitionSpec as P

D = 12288
HEAD_DIM = 128


epsilon = 1e-05


def layer_normed(widened, totals, squares):
    average = totals / D
    variance = squares / D - average * average
    return ((widened - average[:, None]) * lax.rsqrt(variance + epsilon)[:, None]).astype(
        jnp.bfloat16
    )


def attend_piece(query_heads, query_pos, head_count, state, kv_piece, first_row):
    running_max, denominator, weighted = state
    row_count = kv_piece.shape[0]
    head_cols = head_count * HEAD_DIM
    key_heads = kv_piece[:, :head_cols].reshape(row_count, head_count, HEAD_DIM)
    value_heads = kv_piece[:, head_cols:].reshape(row_count, head_count, HEAD_DIM)
    score_scale = 1.0 / HEAD_DIM**0.5
    scores = (
        jnp.einsum("hqd,khd->hqk", query_heads, key_heads, preferred_element_type=jnp.float32)
        * score_scale
    )
    key_pos = first_row + jnp.arange(row_count, dtype=jnp.int32)
    allowed = (query_pos[:, None] >= key_pos[None, :])[None]
    scores = jnp.where(allowed, scores, jnp.float32(-1e30))
    new_max = jnp.maximum(running_max, jnp.max(scores, 2))
    weights = jnp.where(allowed, jnp.exp(scores - new_max[:, :, None]), jnp.float32(0.0))
    factor = jnp.exp(running_max - new_max)
    denominator = denominator * factor + jnp.sum(weights, 2)
    mixed = jnp.einsum(
        "hqk,khd->hqd",
        weights.astype(jnp.bfloat16),
        value_heads,
        preferred_element_type=jnp.float32,
    )
    weighted = weighted * factor[:, :, None] + mixed
    return (new_max, denominator, weighted)


def per_device(activations, qkv_weight, out_weight):
    row_size = lax.axis_size("row")
    col_size = lax.axis_size("col")
    local_rows = activations.shape[0]
    seq_total = local_rows * col_size
    query_rows = seq_total // row_size
    row_width = activations.shape[1]
    head_cols = qkv_weight.shape[2]
    head_count = head_cols // HEAD_DIM
    gathered = lax.all_gather(activations, "col", axis=0, tiled=True)
    widened = gathered.astype(jnp.float32)
    totals, squares = lax.psum((jnp.sum(widened, 1), jnp.sum(widened * widened, 1)), "row")
    normed = layer_normed(widened, totals, squares)
    flat_weight = qkv_weight.reshape(row_width, 3 * head_cols)
    query_pos = lax.axis_index("row") * query_rows + jnp.arange(query_rows, dtype=jnp.int32)
    start_state = (
        jnp.full((head_count, query_rows), -1e30, jnp.float32),
        jnp.zeros((head_count, query_rows), jnp.float32),
        jnp.zeros((head_count, query_rows, HEAD_DIM), jnp.float32),
    )
    row_slice = normed
    queries = lax.psum_scatter(
        jnp.dot(row_slice, flat_weight[:, :head_cols], preferred_element_type=jnp.float32),
        "row",
        scatter_dimension=0,
        tiled=True,
    ).astype(jnp.bfloat16)
    kv_partial = jnp.dot(normed, flat_weight[:, head_cols:], preferred_element_type=jnp.float32)
    keyvals = lax.psum(kv_partial, "row").astype(jnp.bfloat16)
    query_heads = queries.reshape(query_rows, head_count, HEAD_DIM).transpose(1, 0, 2)
    key_block = math.gcd(seq_total, 512)

    def advance(block_index, state_now):
        first_row = (block_index * key_block).astype(jnp.int32)
        kv_piece = lax.dynamic_slice_in_dim(keyvals, first_row, key_block, 0)
        return attend_piece(query_heads, query_pos, head_count, state_now, kv_piece, first_row)

    state = lax.fori_loop(0, seq_total // key_block, advance, start_state)
    running_max, denominator, weighted = state
    attended = (
        (weighted / denominator[:, :, None])
        .transpose(1, 0, 2)
        .reshape(query_rows, head_cols)
        .astype(jnp.bfloat16)
    )
    all_attended = lax.all_gather(attended, "row", axis=0, tiled=True)
    row_slice = all_attended
    return lax.psum_scatter(
        jnp.dot(row_slice, out_weight, preferred_element_type=jnp.float32),
        "col",
        scatter_dimension=0,
        tiled=True,
    ).astype(jnp.bfloat16)


def solution(mesh):
    in_specs = (P("col", "row"), P("row", None, "col"), P("col", "row"))
    out_specs = P("col", "row")
    return jax.shard_map(
        per_device, mesh=mesh, in_specs=in_specs, out_specs=out_specs, check_vma=False
    )
```

profile of v0, /device:TPU:4, one launch (start us, length us, event | category | flops | bytes accessed | tf_op | source)
XLA Modules:
  0.0 992.0 jit_solution(11415254650976039777)
XLA Ops:
  6.5 0.7 all-gather.3.cloned.1.call-update
  7.3 10.3 %copy.9 = bf16[1536,3,768]{0,2,1:T(8,128)(2,1)} copy(bf16[1536,3,768]{2,0,1:T(8,128)(2,1)} %param.6) | data formatting | bytes 14155776 | tf_op args[1]
  17.7 57.1 %all-gather.3.cloned.1.call-done = bf16[2048,1536]{1,0:T(8,128)(2,1)} async-done(((bf16[128,1536]{1,0:T(8,128)(2,1)}), bf16[2048,1536]{1,0:T(8,128)(2,1)}) %all-gather.3.cloned.1.call-update) | async-done | bytes 6291472 | tf_op jit(solution)/shard_map/all_gather | solution.py:60
  74.8 4.6 convert_reduce_fusion
  79.4 33.6 %all-reduce = (f32[2048]{0:T(1024)S(1)}, f32[2048]{0:T(1024)S(1)}) all-reduce(f32[2048]{0:T(1024)S(1)} %get-tuple-element.167, f32[2048]{0:T(1024)S(1)} %get-tuple-element.166), channel_id=1, replica_groups=mesh['row'=8,'col'=16] {'row'}, use_global_device_ids=true, to_apply=%region_3.0 | all-reduce | flops 4096 | bytes 32768 | tf_op jit(solution)/shard_map/psum | solution.py:62
  113.1 16.3 %fusion.18 = f32[2048,1536]{1,0:T(8,128)} fusion(bf16[1536,2304]{0,1:T(8,128)(2,1)} %bitcast.45, bf16[2048,1536]{1,0:T(8,128)(2,1)} %all-gather.3.cloned.1.call-done, f32[2048]{0:T(1024)S(1)} %get-tuple-element.191, f32[2048]{0:T(1024)S(1)} %get-tuple-element.190), kind=kOutput, calls=%fused_computation.27 | convolution fusion | flops 9676259328 | bytes 23609344 | tf_op jit(solution)/shard_map/dot_general | solution.py:78
  129.4 8.7 fusion.20
  138.2 595.0 %all-reduce.2 = bf16[2048,1536]{1,0:T(8,128)(2,1)} all-reduce(f32[2048,1536]{1,0:T(8,128)} %fusion.18), channel_id=1, replica_groups=mesh['row'=8,'col'=16] {'row'}, use_global_device_ids=true, to_apply=%region_4.0 | all-reduce | flops 3145728 | bytes 18874368 | tf_op jit(solution)/shard_map/psum | solution.py:79
  733.2 1.2 convert_element_type.34
  734.4 0.2 copy.10
  734.6 0.9 copy.12
  735.5 45.1 %while.18 = (s32[]{:T(128)}, f32[6,256]{1,0:T(8,128)S(1)}, f32[6,256]{1,0:T(8,128)S(1)}, f32[6,256,128]{2,1,0:T(8,128)}, bf16[2048,1536]{1,0:T(8,128)(2,1)}, /*i...) while((s32[]{:T(128)}, f32[6,256]{1,0:T(8,128)S(1)}, ...), condition=%wide.region_9.10_spmd.clone, body=%wide.region_6.9_spmd.clone.sunk | while | flops 413606144 | bytes 29333796 | solution.py:88
  735.5 0.1 broadcast_compare_fusion.2
  735.7 2.4 fusion.44
  738.0 2.3 copy.22
  740.4 1.2 copy.23
  741.5 2.1 fusion.45
  743.6 0.8 fusion.46
  744.4 1.4 fusion.48
  745.9 0.9 copy-done.4
  746.8 0.1 broadcast_compare_fusion.2
  746.9 2.4 fusion.44
  749.3 2.3 copy.22
  751.6 1.2 copy.23
  752.8 2.1 fusion.45
  754.9 0.8 fusion.46
  755.7 1.4 fusion.48
  757.2 0.9 copy-done.4
  758.2 2.4 fusion.44
  760.6 2.3 copy.22
  762.9 1.2 copy.23
  764.1 2.1 fusion.45
  766.2 0.8 fusion.46
  767.0 1.4 fusion.48
  768.4 0.9 copy-done.4
  769.5 2.4 fusion.44
  771.8 2.3 copy.22
  774.2 1.2 copy.23
  775.3 2.1 fusion.45
  777.4 0.8 fusion.46
  778.2 1.4 fusion.48
  779.7 0.9 copy-done.4
  780.6 1.4 copy.13
  782.0 0.8 divide_convert_fusion
  782.9 68.8 %all-gather.5.cloned.1.call-done = bf16[2048,768]{0,1:T(8,128)(2,1)} async-done(((bf16[256,768]{0,1:T(8,128)(2,1)}), bf16[2048,768]{0,1:T(8,128)(2,1)}) %all-gather.5.cloned.1.call-update) | async-done | bytes 3145744 | tf_op jit(solution)/shard_map/all_gather | solution.py:96
  851.7 10.0 %fusion.25 = f32[2048,1536]{1,0:T(8,128)} fusion(bf16[2048,768]{0,1:T(8,128)(2,1)} %all-gather.5.cloned.1.call-done, bf16[768,1536]{1,0:T(8,128)(2,1)S(1)} %copy-done), kind=kOutput, calls=%fused_computation.35 | convolution fusion | flops 4831838208 | bytes 18087936 | tf_op jit(solution)/shard_map/dot_general | solution.py:99
  861.7 121.8 %reduce-scatter.5.cloned.1.call-done = f32[128,1536]{1,0:T(8,128)} async-done(((f32[2048,1536]{1,0:T(8,128)}), f32[128,1536]{1,0:T(8,128)}) %reduce-scatter.5.cloned.1.call-update) | async-done | bytes 786448 | tf_op jit(solution)/shard_map/reduce_scatter | solution.py:98
  983.6 1.9 convert_element_type.38
  (58 shorter events, 0.6 us)
Async XLA Ops:
  6.5 845.1 %copy-start = (bf16[768,1536]{1,0:T(8,128)(2,1)S(1)}, bf16[768,1536]{1,0:T(8,128)(2,1)}, u32[]{:S(2)}) copy-start(bf16[768,1536]{1,0:T(8,128)(2,1)} %param.7) | copy-start | bytes 7077892
  6.5 68.2 %all-gather.3.cloned.1.call-start = ((), (), s32[]{:S(2)}) async-start(), calls=%async_computation.2 | async-start | bytes 6684672 | tf_op jit(solution)/shard_map/all_gather | solution.py:60
  7.3 726.0 %reduce-scatter.3.cloned.1.call-start = ((), (), s32[]{:S(2)}) async-start(), calls=%async_computation.3 | async-start | bytes 7077888 | tf_op jit(solution)/shard_map/reduce_scatter | solution.py:72
  113.1 16.3 %copy-start.2 = (bf16[2048,1536]{1,0:T(8,128)(2,1)S(1)}, bf16[2048,1536]{1,0:T(8,128)(2,1)}, u32[]{:S(2)}) copy-start(bf16[2048,1536]{1,0:T(8,128)(2,1)} %all-gather.3.cloned.1.call-done) | copy-start | bytes 18874372
  138.1 713.5 %all-gather.5.cloned.1.call-start = ((), (), s32[]{:S(2)}) async-start(), calls=%async_computation.4 | async-start | bytes 3538944 | tf_op jit(solution)/shard_map/all_gather | solution.py:96
  741.5 2.9 copy-start.1
  741.5 2.9 copy-start.3
  745.9 0.9 copy-start.4
  752.8 2.9 copy-start.1
  752.8 2.9 copy-start.3
  757.1 0.9 copy-start.4
  764.1 2.9 copy-start.1
  764.1 2.9 copy-start.3
  768.4 0.9 copy-start.4
  775.3 2.9 copy-start.1
  775.3 2.9 copy-start.3
  779.7 0.9 copy-start.4
  782.8 200.7 %reduce-scatter.5.cloned.1.call-start = ((), (), s32[]{:S(2)}) async-start(), calls=%async_computation.5 | async-start | bytes 13369344 | tf_op jit(solution)/shard_map/reduce_scatter | solution.py:98
Sparse Core Ops, SparseCore 0:
  9.8 64.9 all-gather.2
  138.3 245.8 reduce-scatter.2
  782.9 68.6 all-gather.4
  861.8 121.6 reduce-scatter.4
where the time goes:
time: 995 us; the launch traced here: 992 us
  blocking collectives  629 us (63%)
  waiting for transfers between devices  248 us (25%)
  matrix products  49.1 us (5%)
  local copies, waits for them, and re-layouts  39.8 us (4%)
  between operations  13.2 us (1%)
  other arithmetic  12.3 us (1%)
    psum x1, blocking collectives, per_device(): keyvals = lax.psum(kv_partial, 'row').astype(jnp.bfloat16)  595 us
    reduce_scatter x1, waiting for transfers between devices, per_device(): lax.psum_scatter(jnp.dot(row_slice, out_weight, preferred_element_type=jn...  122 us
    all_gather x1, waiting for transfers between devices, per_device(): all_attended = lax.all_gather(attended, 'row', axis=0, tiled=True)  68.8 us
    all_gather x1, waiting for transfers between devices, per_device(): gathered = lax.all_gather(activations, 'col', axis=0, tiled=True)  57.1 us
    psum x1, blocking collectives, per_device(): lax.psum((jnp.sum(widened, 1), jnp.sum(widened * widened, 1)), 'row')  33.6 us
  transfers between devices with their start and end apart: 4, of which 3 were waited for; matrix products, arithmetic and copies ran while one was open for 1% of the time, Pallas kernels for 0%

commit v1 on v0

v1 whole, which is shorter than its diff:
```python
import functools

import jax
import jax.numpy as jnp
from jax import lax
from jax.experimental import pallas as pl
from jax.experimental.pallas import tpu as pltpu
from jax.sharding import PartitionSpec as P

D = 12288
HEAD_DIM = 128
EPSILON = 1e-05
MESH = pl.DeviceIdType.MESH
F32 = jnp.float32
BF16 = jnp.bfloat16

ARRIVAL = ((0, 0), (0, 1), (1, 0), (3, 0), (2, 0), (1, 1), (3, 1), (2, 1))
Z_FIRST = (True, False, True, False, True, False, True, True)
DEPART = ((2, 1), (2, 0), (1, 1), (3, 1), (1, 0), (3, 0), (0, 1), (0, 0))
SPREAD_Z_FIRST = (True, False, True, False, True, False, True, False)
OTHERS = tuple((dz, dy) for dz in range(4) for dy in range(2) if (dz, dy) != (0, 0))


class Place:
    def __init__(self):
        row = lax.axis_index("row")
        col = lax.axis_index("col")
        self.z, self.y = row // 2, row % 2
        self.x, self.yh, self.core = col // 4, (col // 2) % 2, col % 2

    def device(self, dz=0, dy=0, dx=0, dyh=0, dcore=0):
        row = ((self.z + dz) % 4) * 2 + (self.y + dy) % 2
        col = ((self.x + dx) % 4) * 4 + ((self.yh + dyh) % 2) * 2 + (self.core + dcore) % 2
        return {"row": row, "col": col}

    def level(self, dz):
        return (self.z + dz + 2 * self.core) % 4

    def active(self, dz):
        return self.level(dz) < 3

    def head(self, dz, dy):
        return self.level(dz) * 2 + (self.y + dy) % 2

    def chunk(self, dx, dyh):
        return ((self.x + dx) % 4) * 2 + (self.yh + dyh) % 2


class Traffic:
    def __init__(self, place):
        self.place = place
        self.sent = []

    def send(self, build, level=None):
        def make():
            src, dst, send_sem, recv_sem, target = build()
            return pltpu.make_async_remote_copy(
                src_ref=src,
                dst_ref=dst,
                send_sem=send_sem,
                recv_sem=recv_sem,
                device_id=target,
                device_id_type=MESH,
            )

        make().start()
        self.sent.append((make, level))

    def arrive(self, dst, send_sem, recv_sem):
        pltpu.make_async_remote_copy(
            src_ref=dst,
            dst_ref=dst,
            send_sem=send_sem,
            recv_sem=recv_sem,
            device_id=self.place.device(dcore=1),
            device_id_type=MESH,
        ).wait_recv()

    def drain(self):
        for make, level in self.sent:
            if level is None:
                make().wait_send()
            else:
                pl.when(self.place.active(level))(lambda make=make: make().wait_send())


def greet(place):
    barrier = pltpu.get_barrier_semaphore()
    peers = [place.device(dz=dz, dy=dy) for dz, dy in OTHERS]
    peers += [place.device(dcore=1), place.device(dyh=1)]
    peers += [place.device(dx=dx) for dx in (1, 2, 3)]
    for peer in peers:
        pl.semaphore_signal(barrier, inc=1, device_id=peer, device_id_type=MESH)
    return barrier, len(peers)


def row_tiles(count, tile, body):
    def step(i, carry):
        body(pl.ds(pl.multiple_of(i * tile, tile), tile))
        return carry

    lax.fori_loop(0, count // tile, step, 0)


def project_kernel(
    act_ref, w_ref, qkv_ref,
    wv, nb, pb, yr, ca, zb, st,
    w_sem, st_s, st_r, ag_s, ag_r, y_s, y_r, a_s, a_r, b_s, b_r,
):
    place = Place()
    z, y, core = place.z, place.y, place.core
    traffic = Traffic(place)
    loads = [pltpu.make_async_copy(w_ref.at[k], wv.at[k], w_sem.at[k]) for k in range(3)]
    for load in loads:
        load.start()
    barrier, greeted = greet(place)

    wide = act_ref[...].astype(F32)
    total = jnp.sum(wide, 1, keepdims=True)
    square = jnp.sum(wide * wide, 1, keepdims=True)
    lane = lax.broadcasted_iota(jnp.int32, (128, 128), 1)
    st[0] = jnp.where(lane == 0, total, square).T[0:8]
    pl.semaphore_wait(barrier, greeted)
    for dz, dy in OTHERS:
        slot = ((4 - dz) % 4) * 2 + dy
        traffic.send(
            lambda slot=slot, dz=dz, dy=dy: (
                st.at[0], st.at[slot], st_s.at[slot], st_r.at[slot], place.device(dz=dz, dy=dy)
            )
        )
    for slot in range(1, 8):
        traffic.arrive(st.at[slot], st_s.at[slot], st_r.at[slot])
    sums = st[0]
    for slot in range(1, 8):
        sums = sums + st[slot]
    turned = jnp.concatenate([sums] * 16, axis=0).T
    average = turned[:, 0:1] / D
    variance = turned[:, 1:2] / D - average * average
    scale = lax.rsqrt(variance + EPSILON)
    nb[0, 0, core] = ((act_ref[...].astype(F32) - average) * scale).astype(BF16)

    used = []

    def share(dx, dyh, ex, eyh, ecore):
        rx, ryh, count = (dx - ex) % 4, (dyh + eyh) % 2, len(used)
        traffic.send(
            lambda: (
                nb.at[dx, dyh, core],
                nb.at[rx, ryh, core],
                ag_s.at[count],
                ag_r.at[rx, ryh, core],
                place.device(dx=ex, dyh=eyh, dcore=ecore),
            )
        )
        used.append(0)

    share(0, 0, 0, 0, 1)
    share(0, 0, 0, 1, 0)
    for ex in (1, 3, 2):
        share(0, 0, ex, 0, 0)

    def receive(dx, dyh, of):
        traffic.arrive(nb.at[dx, dyh, of], ag_s.at[0], ag_r.at[dx, dyh, of])

    def stage_gather(step):
        dx, dyh = ARRIVAL[step]
        if step:
            receive(dx, dyh, core)
            share(dx, dyh, 0, 0, 1)
            if (dx, dyh) == (0, 1):
                for ex in (1, 3, 2):
                    share(0, 1, ex, 0, 0)
        receive(dx, dyh, 1 - core)

    def stage_project(step):
        dx, dyh = ARRIVAL[step]

        def tile(i, carry):
            kind, level = i // 3, i % 3
            columns = pl.ds(pl.multiple_of(level * 256, 256), 256)
            part = jnp.dot(
                nb[dx, dyh].reshape(256, 1536), wv[kind, :, columns], preferred_element_type=F32
            ).astype(BF16)
            dz = (level + 8 - 2 * core - z) % 4
            where = pl.ds(pl.multiple_of(kind * 128, 128), 128)
            for side in range(2):
                pb[step, dz, (side + y) % 2, :, where] = part[:, side * 128 : side * 128 + 128]
            return carry

        lax.fori_loop(0, 9, tile, 0)

    def sides(step):
        return pl.ds(0, 2 if Z_FIRST[step] else 1)

    def send_y(step, dz):
        traffic.send(
            lambda: (
                pb.at[step, dz, 1], yr.at[step, dz], y_s.at[step, dz], y_r.at[step, dz],
                place.device(dy=1),
            ),
            dz,
        )

    def arrive_y(step, dz):
        traffic.arrive(yr.at[step, dz], y_s.at[step, dz], y_r.at[step, dz])

    def z_far(step):
        def go():
            for way, hop in ((0, 1), (1, 3)):
                traffic.send(
                    lambda way=way, hop=hop: (
                        pb.at[step, 2, sides(step), pl.ds(way * 128, 128)],
                        ca.at[step, way, sides(step)],
                        a_s.at[step, way],
                        a_r.at[step, way],
                        place.device(dz=hop),
                    ),
                    2,
                )

        pl.when(place.active(2))(go)

    def z_near(step):
        for way, hop in ((0, 1), (1, 3)):

            def go(way=way, hop=hop):
                traffic.arrive(ca.at[step, way, sides(step)], a_s.at[step, way], a_r.at[step, way])
                for side in range(2 if Z_FIRST[step] else 1):

                    def add(rows, side=side):
                        at = pl.ds(pl.multiple_of(rows.start + way * 128, 32), 32)
                        pb[step, hop, side, at, :] = (
                            pb[step, hop, side, at, :].astype(F32)
                            + ca[step, way, side, rows, :].astype(F32)
                        ).astype(BF16)

                    row_tiles(128, 32, add)
                traffic.send(
                    lambda: (
                        pb.at[step, hop, sides(step)], zb.at[step, way, sides(step)],
                        b_s.at[step, way], b_r.at[step, way], place.device(dz=hop),
                    ),
                    hop,
                )

            pl.when(place.active(hop))(go)

    def arrive_near(step):
        for way in range(2):
            traffic.arrive(zb.at[step, way, sides(step)], b_s.at[step, way], b_r.at[step, way])

    def finish(step):
        t = place.chunk(*ARRIVAL[step])

        def add(rows):
            at = pl.ds(pl.multiple_of(rows.start + t * 256, 32), 32)
            qkv_ref[at, :] = (
                pb[step, 0, 0, rows, :].astype(F32)
                + yr[step, 0, rows, :].astype(F32)
                + zb[step, 0, 0, rows, :].astype(F32)
                + zb[step, 1, 0, rows, :].astype(F32)
            ).astype(BF16)

        row_tiles(256, 32, add)

    def stage_a(step):
        stage_gather(step)
        if step == 0:
            for load in loads:
                load.wait()
        stage_project(step)
        if Z_FIRST[step]:
            z_far(step)
        else:
            for dz in (2, 1, 3, 0):
                pl.when(place.active(dz))(functools.partial(send_y, step, dz))

    def stage_b(step):
        if Z_FIRST[step]:
            z_near(step)
            return
        for dz in (2, 1, 3):

            def go(dz=dz):
                arrive_y(step, dz)

                def add(rows):
                    pb[step, dz, 0, rows, :] = (
                        pb[step, dz, 0, rows, :].astype(F32) + yr[step, dz, rows, :].astype(F32)
                    ).astype(BF16)

                row_tiles(256, 32, add)

            pl.when(place.active(dz))(go)
            if dz == 2:
                z_far(step)

    def stage_c(step):
        if not Z_FIRST[step]:
            z_near(step)
            return

        def go():
            arrive_near(step)

            def add(rows):
                pb[step, 0, 1, rows, :] = (
                    pb[step, 0, 1, rows, :].astype(F32)
                    + zb[step, 0, 1, rows, :].astype(F32)
                    + zb[step, 1, 1, rows, :].astype(F32)
                ).astype(BF16)

            row_tiles(256, 32, add)
            send_y(step, 0)

        pl.when(place.active(0))(go)

    def stage_d(step):
        def go():
            if not Z_FIRST[step]:
                arrive_near(step)
            arrive_y(step, 0)
            finish(step)

        pl.when(place.active(0))(go)

    for turn in range(11):
        for lag, stage in enumerate((stage_a, stage_b, stage_c, stage_d)):
            if 0 <= turn - lag < 8:
                stage(turn - lag)
    traffic.drain()


def attend_kernel(
    qkv_ref, wo_ref, out_ref,
    wv, at, score, acc, cs, cr, pb, ca, xb, yr,
    w_sem, t_s, t_r, c_s, c_r, a_s, a_r, b_s, b_r, y_s, y_r,
):
    place = Place()
    core = place.core
    traffic = Traffic(place)
    load = pltpu.make_async_copy(wo_ref, wv, w_sem)
    load.start()
    barrier, greeted = greet(place)
    pl.semaphore_wait(barrier, greeted)
    factor = 1.4426950408889634 / HEAD_DIM**0.5

    def head_columns(dz, dy):
        return pl.ds(pl.multiple_of(place.head(dz, dy) * 128, 128), 128)

    def piece(step, dz, dy):
        return at.at[step, :, head_columns(dz, dy)]

    def attend(step):
        t = place.chunk(*DEPART[step])
        query = qkv_ref[pl.ds(pl.multiple_of(t * 256, 256), 256), 0:128]

        def block(j):
            return pl.ds(pl.multiple_of(j * 256, 256), 256)

        def scores(j):
            return lax.dot_general(
                query, qkv_ref[block(j), 128:256], (((1,), (1,)), ((), ())),
                preferred_element_type=F32,
            )

        def first(j, top):
            now = scores(j)
            score[:, block(j)] = now
            return jnp.maximum(top, jnp.maximum(now[:, :128], now[:, 128:]))

        row = lax.broadcasted_iota(jnp.int32, (256, 256), 0)
        col = lax.broadcasted_iota(jnp.int32, (256, 256), 1)
        now = jnp.where(row >= col, scores(t), F32(-1e30))
        score[:, block(t)] = now
        top = lax.fori_loop(0, t, first, jnp.maximum(now[:, :128], now[:, 128:]))
        top = jnp.max(top, 1, keepdims=True)

        def second(j, state):
            low, mixed = state
            weight = jnp.exp2((score[:, block(j)] - top) * factor)
            low = low + (weight[:, :128] + weight[:, 128:])
            mixed = mixed + jnp.dot(
                weight.astype(BF16), qkv_ref[block(j), 256:384], preferred_element_type=F32
            )
            return low, mixed

        zero = jnp.zeros((256, 128), F32)
        low, mixed = lax.fori_loop(0, t + 1, second, (zero, zero))
        at[step, :, head_columns(0, 0)] = (mixed / jnp.sum(low, 1, keepdims=True)).astype(BF16)

    spread = []

    def share(step, dz, dy, ez, ey):
        rz, ry = (dz - ez) % 4, (dy + ey) % 2
        count = sum(1 for s in spread if s == step)
        spread.append(step)
        traffic.send(
            lambda: (
                piece(step, dz, dy), piece(step, dz, dy), t_s.at[step, count],
                t_r.at[step, rz, ry], place.device(dz=ez, dy=ey),
            ),
            dz,
        )

    def receive(step, dz, dy):
        traffic.arrive(piece(step, dz, dy), t_s.at[step, 0], t_r.at[step, dz, dy])

    def stage_a(step):
        def go():
            attend(step)
            share(step, 0, 0, 0, 1)
            for ez in (2, 1, 3):
                share(step, 0, 0, ez, 0)

        pl.when(place.active(0))(go)

    def stage_b(step):
        if SPREAD_Z_FIRST[step]:
            for dz in (1, 3, 2):

                def go(dz=dz):
                    receive(step, dz, 0)
                    share(step, dz, 0, 0, 1)

                pl.when(place.active(dz))(go)
        else:

            def go():
                receive(step, 0, 1)
                for ez in (2, 1, 3):
                    share(step, 0, 1, ez, 0)

            pl.when(place.active(0))(go)

    def stage_c(step):
        if step == 0:
            load.wait()
        for dz, dy in OTHERS:
            done = dy == 0 and dz > 0 if SPREAD_Z_FIRST[step] else (dz, dy) == (0, 1)
            if not done:
                pl.when(place.active(dz))(functools.partial(receive, step, dz, dy))

        def half(which):
            return at[step, pl.ds(pl.multiple_of(which * 128, 128), 128), :]

        def theirs(i, carry):
            columns = pl.ds(pl.multiple_of(i * 256, 256), 256)
            cs[step, :, columns] = jnp.dot(
                half(1 - core), wv[:, columns], preferred_element_type=F32
            ).astype(BF16)
            return carry

        lax.fori_loop(0, 6, theirs, 0)
        traffic.send(
            lambda: (cs.at[step], cr.at[step], c_s.at[step], c_r.at[step], place.device(dcore=1))
        )

        def mine(i, carry):
            columns = pl.ds(pl.multiple_of(i * 256, 256), 256)
            acc[step % 2, :, columns] = jnp.dot(
                half(core), wv[:, columns], preferred_element_type=F32
            )
            return carry

        lax.fori_loop(0, 6, mine, 0)

    def stage_d(step):
        dx, dyh = DEPART[step]
        traffic.arrive(cr.at[step], c_s.at[step], c_r.at[step])
        way = {1: 0, 3: 1}.get(dx)
        if way is not None:
            traffic.arrive(ca.at[dyh, way], a_s.at[dyh, way], a_r.at[dyh, way])
        if dx == 0:
            for w in range(2):
                traffic.arrive(xb.at[dyh, w], b_s.at[dyh, w], b_r.at[dyh, w])
            if dyh == 0:
                traffic.arrive(yr, y_s, y_r)

        def combine(lo):
            def add(rows):
                here = pl.ds(pl.multiple_of(rows.start + lo * 64, 16), 16)
                now = acc[step % 2, here, :] + cr[step, here, :].astype(F32)
                if way is not None and lo == way:
                    now = now + ca[dyh, way, rows, :].astype(F32)
                if dx == 0:
                    now = now + xb[dyh, 0, here, :].astype(F32) + xb[dyh, 1, here, :].astype(F32)
                if (dx, dyh) == (0, 0):
                    out_ref[here, :] = (now + yr[here, :].astype(F32)).astype(BF16)
                else:
                    pb[dx, dyh, here, :] = now.astype(BF16)

            row_tiles(64, 16, add)

        combine(0)
        combine(1)
        if dx == 2:
            for w, hop in ((0, 1), (1, 3)):
                traffic.send(
                    lambda w=w, hop=hop: (
                        pb.at[2, dyh, pl.ds(w * 64, 64)], ca.at[dyh, w], a_s.at[dyh, w],
                        a_r.at[dyh, w], place.device(dx=hop),
                    )
                )
        elif way is not None:
            traffic.send(
                lambda: (
                    pb.at[dx, dyh], xb.at[dyh, way], b_s.at[dyh, way], b_r.at[dyh, way],
                    place.device(dx=dx),
                )
            )
        elif dyh == 1:
            traffic.send(lambda: (pb.at[0, 1], yr, y_s, y_r, place.device(dyh=1)))

    for turn in range(11):
        for lag, stage in enumerate((stage_a, stage_b, stage_c, stage_d)):
            if 0 <= turn - lag < 8:
                stage(turn - lag)
    traffic.drain()


def dma(*shape):
    return pltpu.SemaphoreType.DMA(shape) if shape else pltpu.SemaphoreType.DMA


def project(activations, weight):
    return pl.pallas_call(
        project_kernel,
        out_shape=jax.ShapeDtypeStruct((2048, 384), BF16),
        in_specs=[pl.BlockSpec(memory_space=pltpu.VMEM), pl.BlockSpec(memory_space=pl.ANY)],
        out_specs=pl.BlockSpec(memory_space=pltpu.VMEM),
        scratch_shapes=[
            pltpu.VMEM((3, 1536, 768), BF16),
            pltpu.VMEM((4, 2, 2, 128, 1536), BF16),
            pltpu.VMEM((8, 4, 2, 256, 384), BF16),
            pltpu.VMEM((8, 4, 256, 384), BF16),
            pltpu.VMEM((8, 2, 2, 128, 384), BF16),
            pltpu.VMEM((8, 2, 2, 256, 384), BF16),
            pltpu.VMEM((8, 8, 128), F32),
            dma(3), dma(8), dma(8), dma(16), dma(4, 2, 2), dma(8, 4), dma(8, 4),
            dma(8, 2), dma(8, 2), dma(8, 2), dma(8, 2),
        ],
        compiler_params=pltpu.CompilerParams(
            collective_id=1, has_side_effects=True, vmem_limit_bytes=56 << 20
        ),
        name="project",
    )(activations, weight)


def attend(qkv, weight):
    return pl.pallas_call(
        attend_kernel,
        out_shape=jax.ShapeDtypeStruct((128, 1536), BF16),
        in_specs=[pl.BlockSpec(memory_space=pltpu.VMEM), pl.BlockSpec(memory_space=pl.ANY)],
        out_specs=pl.BlockSpec(memory_space=pltpu.VMEM),
        scratch_shapes=[
            pltpu.VMEM((768, 1536), BF16),
            pltpu.VMEM((8, 256, 768), BF16),
            pltpu.VMEM((256, 2048), F32),
            pltpu.VMEM((2, 128, 1536), F32),
            pltpu.VMEM((8, 128, 1536), BF16),
            pltpu.VMEM((8, 128, 1536), BF16),
            pltpu.VMEM((4, 2, 128, 1536), BF16),
            pltpu.VMEM((2, 2, 64, 1536), BF16),
            pltpu.VMEM((2, 2, 128, 1536), BF16),
            pltpu.VMEM((128, 1536), BF16),
            dma(), dma(8, 8), dma(8, 4, 2), dma(8), dma(8),
            dma(2, 2), dma(2, 2), dma(2, 2), dma(2, 2), dma(), dma(),
        ],
        compiler_params=pltpu.CompilerParams(
            collective_id=2, has_side_effects=True, vmem_limit_bytes=56 << 20
        ),
        name="attend",
    )(qkv, weight)


def per_device(activations, qkv_weight, out_weight):
    qkv = project(activations, jnp.transpose(qkv_weight, (1, 0, 2)))
    return attend(qkv, out_weight)


def solution(mesh):
    in_specs = (P("col", "row"), P("row", None, "col"), P("col", "row"))
    return jax.shard_map(
        per_device, mesh=mesh, in_specs=in_specs, out_specs=P("col", "row"), check_vma=False
    )
```

time: 995 us -> 181 us (0.18)
  blocking collectives: 629 us -> 0 us
  waiting for transfers between devices: 248 us -> 0 us
  Pallas kernels: 0 us -> 179 us
  matrix products: 49.1 us -> 0 us
  local copies, waits for them, and re-layouts: 39.8 us -> 1.77 us
  between operations: 13.2 us -> 0.02 us
  other arithmetic: 12.3 us -> 0 us
    psum x2 -> x0, blocking collectives: 629 us -> none  [the longest x1 595 us: per_device(): keyvals = lax.psum(kv_partial, 'row').astype(jnp.bfloat16)]
    pallas_call x0 -> x2, Pallas kernels: none -> 179 us  [the longest x1 114 us: project(): pl.pallas_call(project_kernel, out_shape=jax.ShapeDtypeStruct((2048, 384)...]
    all_gather x2 -> x0, waiting for transfers between devices: 126 us -> none  [the longest x1 68.8 us: per_device(): all_attended = lax.all_gather(attended, 'row', axis=0, tiled=True)]
    reduce_scatter x2 -> x0, waiting for transfers between devices: 122 us -> none  [the longest x1 122 us: per_device(): lax.psum_scatter(jnp.dot(row_slice, out_weight, preferred_element_type=jn...]
    dot_general x11 -> x0, matrix products: 49.1 us -> none  [the longest x1 16.3 us: per_device(): jnp.dot(normed, flat_weight[:, head_cols:], preferred_element_type=jnp.fl...]
    while x37 -> x0, local copies, waits for them, and re-layouts: 18.9 us -> none
  transfers between devices with their start and end apart: 4 -> 0, of which waited for: 3 -> 0; matrix products, arithmetic and copies ran while one was open for 1% -> 0% of each run, Pallas kernels for 0% -> 0%
where the time goes in v1:
time: 181 us
  Pallas kernels  179 us (99%)
    pallas_call x1, Pallas kernels, project(): pl.pallas_call(project_kernel, out_shape=jax.ShapeDtypeStruct((2048, 384)...  114 us
    pallas_call x1, Pallas kernels, attend(): pl.pallas_call(attend_kernel, out_shape=jax.ShapeDtypeStruct((128, 1536),...  64.8 us

profile of v1, /device:TPU:4, one launch (start us, length us, event | category | flops | bytes accessed | tf_op | source)
XLA Modules:
  0.0 180.9 jit_solution(3244178447036410077)
XLA Ops:
  0.0 114.3 %project.1.qkv_ref = bf16[2048,384]{1,0:T(8,128)(2,1)} custom-call(bf16[128,1536]{1,0:T(8,128)(2,1)} %act_ref.1, bf16[3,1536,768]{2,1,0:T(8,128)(2,1)} %bitcast.1), custom_call_target="tpu_custom_call" | custom-call | tf_op jit(solution)/shard_map/project/pallas_call | solution.py:527
  114.3 64.8 %attend.1 = bf16[128,1536]{1,0:T(8,128)(2,1)} custom-call(bf16[2048,384]{1,0:T(8,128)(2,1)} %project.1.qkv_ref, bf16[768,1536]{1,0:T(8,128)(2,1)} %wo_ref.1), custom_call_target="tpu_custom_call" | custom-call | tf_op jit(solution)/shard_map/attend/pallas_call | solution.py:551
  179.2 1.8 copy.5

commit v2 on v1

--- a/solution.py
+++ b/solution.py
@@ -15,8 +15,11 @@
 BF16 = jnp.bfloat16
 
 ARRIVAL = ((0, 0), (0, 1), (1, 0), (3, 0), (2, 0), (1, 1), (3, 1), (2, 1))
-Z_FIRST = (True, False, True, False, True, False, True, True)
-DEPART = ((2, 1), (2, 0), (1, 1), (3, 1), (1, 0), (3, 0), (0, 1), (0, 0))
+PROJECT_LAGS = (0, 1, 2, 3)
+ATTEND_LAGS = (0, 1, 2, 3, 4)
+ZY = (0, 128, 64)
+YZ = (128, 128, 64)
+DEPART = ((2, 1), (1, 1), (3, 1), (2, 0), (0, 1), (1, 0), (3, 0), (0, 0))
 SPREAD_Z_FIRST = (True, False, True, False, True, False, True, False)
 OTHERS = tuple((dz, dy) for dz in range(4) for dy in range(2) if (dz, dy) != (0, 0))
 
@@ -102,16 +105,26 @@
     lax.fori_loop(0, count // tile, step, 0)
 
 
-def project_kernel(
-    act_ref, w_ref, qkv_ref,
-    wv, nb, pb, yr, ca, zb, st,
-    w_sem, st_s, st_r, ag_s, ag_r, y_s, y_r, a_s, a_r, b_s, b_r,
+def schedule(lags, stages, opening=()):
+    done = set()
+    order = list(opening)
+    for turn in range(8 + max(lags)):
+        order += [(i, turn - lag) for i, lag in enumerate(lags) if 0 <= turn - lag < 8]
+    for i, step in order:
+        if (i, step) not in done:
+            done.add((i, step))
+            stages[i](step)
+
+
+def project(
+    place, traffic, act_ref, w_ref, wo_ref, wov, qkv,
+    wv, nb, pb, yrz, yry, caz, cay, zbz, zby, st,
+    w_sem, st_s, st_r, ag_s, ag_r, yz_s, yz_r, y_s, y_r, a_s, a_r, b_s, b_r,
 ):
-    place = Place()
     z, y, core = place.z, place.y, place.core
-    traffic = Traffic(place)
     loads = [pltpu.make_async_copy(w_ref.at[k], wv.at[k], w_sem.at[k]) for k in range(3)]
-    for load in loads:
+    out_load = pltpu.make_async_copy(wo_ref, wov, w_sem.at[3])
+    for load in [*loads, out_load]:
         load.start()
     barrier, greeted = greet(place)
 
@@ -154,10 +167,23 @@
         )
         used.append(0)
 
+    share(0, 0, 0, 1, 0)
+    for ex in (1, 3):
+        share(0, 0, ex, 0, 0)
     share(0, 0, 0, 0, 1)
-    share(0, 0, 0, 1, 0)
-    for ex in (1, 3, 2):
-        share(0, 0, ex, 0, 0)
+
+    def relay(dyh):
+        count = len(used)
+        traffic.send(
+            lambda: (
+                nb.at[3 - 2 * core, dyh, core],
+                nb.at[2, dyh, core],
+                ag_s.at[count],
+                ag_r.at[2, dyh, core],
+                place.device(dx=1 + 2 * core),
+            )
+        )
+        used.append(0)
 
     def receive(dx, dyh, of):
         traffic.arrive(nb.at[dx, dyh, of], ag_s.at[0], ag_r.at[dx, dyh, of])
@@ -166,10 +192,12 @@
         dx, dyh = ARRIVAL[step]
         if step:
             receive(dx, dyh, core)
+            if (dx, dyh) == (0, 1):
+                for ex in (1, 3):
+                    share(0, 1, ex, 0, 0)
+            if dx == 3:
+                relay(dyh)
             share(dx, dyh, 0, 0, 1)
-            if (dx, dyh) == (0, 1):
-                for ex in (1, 3, 2):
-                    share(0, 1, ex, 0, 0)
         receive(dx, dyh, 1 - core)
 
     def stage_project(step):
@@ -189,79 +217,79 @@
 
         lax.fori_loop(0, 9, tile, 0)
 
-    def sides(step):
-        return pl.ds(0, 2 if Z_FIRST[step] else 1)
+    def rows_of(part, way):
+        low, count, first = part
+        return pl.ds(low, first) if way == 0 else pl.ds(low + first, count - first)
+
+    def z_far(part, step):
+        both = part is ZY
+        for way, hop in ((0, 1), (1, 3)):
+            rows = rows_of(part, way)
+            into = pl.ds(0, rows.size)
+            traffic.send(
+                lambda way=way, hop=hop, rows=rows, into=into: (
+                    pb.at[step, 2, :, rows] if both else pb.at[step, 2, 0, rows],
+                    caz.at[step, way, :, into] if both else cay.at[step, way, into],
+                    a_s.at[int(both), step, way],
+                    a_r.at[int(both), step, way],
+                    place.device(dz=hop),
+                ),
+                2,
+            )
+
+    def z_near(part, step):
+        both = part is ZY
+        for way, hop in ((0, 1), (1, 3)):
+
+            def go(way=way, hop=hop):
+                rows = rows_of(part, way)
+                into = pl.ds(0, rows.size)
+                traffic.arrive(
+                    caz.at[step, way, :, into] if both else cay.at[step, way, into],
+                    a_s.at[int(both), step, way],
+                    a_r.at[int(both), step, way],
+                )
+                for side in range(2 if both else 1):
+
+                    def add(tile, side=side):
+                        here = pl.ds(pl.multiple_of(tile.start + rows.start, 16), 16)
+                        far = caz[step, way, side, tile, :] if both else cay[step, way, tile, :]
+                        pb[step, hop, side, here, :] = (
+                            pb[step, hop, side, here, :].astype(F32) + far.astype(F32)
+                        ).astype(BF16)
+
+                    row_tiles(rows.size, 16, add)
+                whole = pl.ds(part[0], part[1])
+                traffic.send(
+                    lambda: (
+                        pb.at[step, hop, :, whole] if both else pb.at[step, hop, 0, whole],
+                        zbz.at[step, way] if both else zby.at[step, way],
+                        b_s.at[int(both), step, way],
+                        b_r.at[int(both), step, way],
+                        place.device(dz=hop),
+                    ),
+                    hop,
+                )
+
+            pl.when(place.active(hop))(go)
+
+    def arrive_near(part, step):
+        both = part is ZY
+        for way in range(2):
+            traffic.arrive(
+                zbz.at[step, way] if both else zby.at[step, way],
+                b_s.at[int(both), step, way],
+                b_r.at[int(both), step, way],
+            )
 
     def send_y(step, dz):
         traffic.send(
             lambda: (
-                pb.at[step, dz, 1], yr.at[step, dz], y_s.at[step, dz], y_r.at[step, dz],
-                place.device(dy=1),
+                pb.at[step, dz, 1, pl.ds(YZ[0], YZ[1])], yry.at[step, dz], y_s.at[step, dz],
+                y_r.at[step, dz], place.device(dy=1),
             ),
             dz,
         )
-
-    def arrive_y(step, dz):
-        traffic.arrive(yr.at[step, dz], y_s.at[step, dz], y_r.at[step, dz])
-
-    def z_far(step):
-        def go():
-            for way, hop in ((0, 1), (1, 3)):
-                traffic.send(
-                    lambda way=way, hop=hop: (
-                        pb.at[step, 2, sides(step), pl.ds(way * 128, 128)],
-                        ca.at[step, way, sides(step)],
-                        a_s.at[step, way],
-                        a_r.at[step, way],
-                        place.device(dz=hop),
-                    ),
-                    2,
-                )
-
-        pl.when(place.active(2))(go)
-
-    def z_near(step):
-        for way, hop in ((0, 1), (1, 3)):
-
-            def go(way=way, hop=hop):
-                traffic.arrive(ca.at[step, way, sides(step)], a_s.at[step, way], a_r.at[step, way])
-                for side in range(2 if Z_FIRST[step] else 1):
-
-                    def add(rows, side=side):
-                        at = pl.ds(pl.multiple_of(rows.start + way * 128, 32), 32)
-                        pb[step, hop, side, at, :] = (
-                            pb[step, hop, side, at, :].astype(F32)
-                            + ca[step, way, side, rows, :].astype(F32)
-                        ).astype(BF16)
-
-                    row_tiles(128, 32, add)
-                traffic.send(
-                    lambda: (
-                        pb.at[step, hop, sides(step)], zb.at[step, way, sides(step)],
-                        b_s.at[step, way], b_r.at[step, way], place.device(dz=hop),
-                    ),
-                    hop,
-                )
-
-            pl.when(place.active(hop))(go)
-
-    def arrive_near(step):
-        for way in range(2):
-            traffic.arrive(zb.at[step, way, sides(step)], b_s.at[step, way], b_r.at[step, way])
-
-    def finish(step):
-        t = place.chunk(*ARRIVAL[step])
-
-        def add(rows):
-            at = pl.ds(pl.multiple_of(rows.start + t * 256, 32), 32)
-            qkv_ref[at, :] = (
-                pb[step, 0, 0, rows, :].astype(F32)
-                + yr[step, 0, rows, :].astype(F32)
-                + zb[step, 0, 0, rows, :].astype(F32)
-                + zb[step, 1, 0, rows, :].astype(F32)
-            ).astype(BF16)
-
-        row_tiles(256, 32, add)
 
     def stage_a(step):
         stage_gather(step)
@@ -269,80 +297,93 @@
             for load in loads:
                 load.wait()
         stage_project(step)
-        if Z_FIRST[step]:
-            z_far(step)
-        else:
-            for dz in (2, 1, 3, 0):
-                pl.when(place.active(dz))(functools.partial(send_y, step, dz))
+        pl.when(place.active(2))(functools.partial(z_far, ZY, step))
+        for dz in (2, 1, 3, 0):
+            pl.when(place.active(dz))(functools.partial(send_y, step, dz))
 
     def stage_b(step):
-        if Z_FIRST[step]:
-            z_near(step)
-            return
+        z_near(ZY, step)
         for dz in (2, 1, 3):
 
             def go(dz=dz):
-                arrive_y(step, dz)
-
-                def add(rows):
-                    pb[step, dz, 0, rows, :] = (
-                        pb[step, dz, 0, rows, :].astype(F32) + yr[step, dz, rows, :].astype(F32)
+                traffic.arrive(yry.at[step, dz], y_s.at[step, dz], y_r.at[step, dz])
+
+                def add(tile):
+                    here = pl.ds(pl.multiple_of(tile.start + YZ[0], 16), 16)
+                    pb[step, dz, 0, here, :] = (
+                        pb[step, dz, 0, here, :].astype(F32) + yry[step, dz, tile, :].astype(F32)
                     ).astype(BF16)
 
-                row_tiles(256, 32, add)
+                row_tiles(YZ[1], 16, add)
+                if dz == 2:
+                    z_far(YZ, step)
 
             pl.when(place.active(dz))(go)
-            if dz == 2:
-                z_far(step)
 
     def stage_c(step):
-        if not Z_FIRST[step]:
-            z_near(step)
-            return
+        z_near(YZ, step)
 
         def go():
-            arrive_near(step)
-
-            def add(rows):
-                pb[step, 0, 1, rows, :] = (
-                    pb[step, 0, 1, rows, :].astype(F32)
-                    + zb[step, 0, 1, rows, :].astype(F32)
-                    + zb[step, 1, 1, rows, :].astype(F32)
+            arrive_near(ZY, step)
+
+            def add(tile):
+                pb[step, 0, 1, tile, :] = (
+                    pb[step, 0, 1, tile, :].astype(F32)
+                    + zbz[step, 0, 1, tile, :].astype(F32)
+                    + zbz[step, 1, 1, tile, :].astype(F32)
                 ).astype(BF16)
 
-            row_tiles(256, 32, add)
-            send_y(step, 0)
+            row_tiles(ZY[1], 16, add)
+            traffic.send(
+                lambda: (
+                    pb.at[step, 0, 1, pl.ds(ZY[0], ZY[1])], yrz.at[step], yz_s.at[step],
+                    yz_r.at[step], place.device(dy=1),
+                ),
+                0,
+            )
 
         pl.when(place.active(0))(go)
 
     def stage_d(step):
+        t = place.chunk(*ARRIVAL[step])
+
         def go():
-            if not Z_FIRST[step]:
-                arrive_near(step)
-            arrive_y(step, 0)
-            finish(step)
+            arrive_near(YZ, step)
+            traffic.arrive(yry.at[step, 0], y_s.at[step, 0], y_r.at[step, 0])
+            traffic.arrive(yrz.at[step], yz_s.at[step], yz_r.at[step])
+
+            def finish(low, yr, zb0, zb1):
+                def add(tile):
+                    mine = pl.ds(pl.multiple_of(tile.start + low, 16), 16)
+                    here = pl.ds(pl.multiple_of(tile.start + low + t * 256, 16), 16)
+                    qkv[here, :] = (
+                        pb[step, 0, 0, mine, :].astype(F32)
+                        + yr[tile, :].astype(F32)
+                        + zb0[tile, :].astype(F32)
+                        + zb1[tile, :].astype(F32)
+                    ).astype(BF16)
+
+                return add
+
+            row_tiles(
+                ZY[1], 16, finish(ZY[0], yrz.at[step], zbz.at[step, 0, 0], zbz.at[step, 1, 0])
+            )
+            row_tiles(
+                YZ[1], 16, finish(YZ[0], yry.at[step, 0], zby.at[step, 0], zby.at[step, 1])
+            )
 
         pl.when(place.active(0))(go)
 
-    for turn in range(11):
-        for lag, stage in enumerate((stage_a, stage_b, stage_c, stage_d)):
-            if 0 <= turn - lag < 8:
-                stage(turn - lag)
-    traffic.drain()
-
-
-def attend_kernel(
-    qkv_ref, wo_ref, out_ref,
+    schedule(PROJECT_LAGS, (stage_a, stage_b, stage_c, stage_d))
+    return out_load
+
+
+def attend_all(
+    place, traffic, out_load, qkv_ref, out_ref,
     wv, at, score, acc, cs, cr, pb, ca, xb, yr,
-    w_sem, t_s, t_r, c_s, c_r, a_s, a_r, b_s, b_r, y_s, y_r,
+    t_s, t_r, c_s, c_r, a_s, a_r, b_s, b_r, y_s, y_r,
 ):
-    place = Place()
     core = place.core
-    traffic = Traffic(place)
-    load = pltpu.make_async_copy(wo_ref, wv, w_sem)
-    load.start()
-    barrier, greeted = greet(place)
-    pl.semaphore_wait(barrier, greeted)
     factor = 1.4426950408889634 / HEAD_DIM**0.5
 
     def head_columns(dz, dy):
@@ -406,21 +447,26 @@
     def receive(step, dz, dy):
         traffic.arrive(piece(step, dz, dy), t_s.at[step, 0], t_r.at[step, dz, dy])
 
+    def relay(step):
+        return 1 if (step // 2) % 2 == 0 else 3
+
     def stage_a(step):
         def go():
             attend(step)
-            share(step, 0, 0, 0, 1)
-            for ez in (2, 1, 3):
-                share(step, 0, 0, ez, 0)
+            for ez, ey in ((1, 0), (3, 0), (0, 1)):
+                share(step, 0, 0, ez, ey)
 
         pl.when(place.active(0))(go)
 
     def stage_b(step):
+        onward = relay(step)
         if SPREAD_Z_FIRST[step]:
-            for dz in (1, 3, 2):
+            for dz in (4 - onward, onward):
 
                 def go(dz=dz):
                     receive(step, dz, 0)
+                    if dz == 4 - onward:
+                        share(step, dz, 0, onward, 0)
                     share(step, dz, 0, 0, 1)
 
                 pl.when(place.active(dz))(go)
@@ -428,16 +474,37 @@
 
             def go():
                 receive(step, 0, 1)
-                for ez in (2, 1, 3):
+                for ez in (1, 3):
                     share(step, 0, 1, ez, 0)
 
             pl.when(place.active(0))(go)
 
     def stage_c(step):
+        onward = relay(step)
+        if SPREAD_Z_FIRST[step]:
+
+            def go():
+                receive(step, 2, 0)
+                share(step, 2, 0, 0, 1)
+
+            pl.when(place.active(2))(go)
+        else:
+
+            def go():
+                for dy in range(2):
+                    receive(step, 4 - onward, dy)
+                    share(step, 4 - onward, dy, onward, 0)
+
+            pl.when(place.active(4 - onward))(go)
+
+    def stage_d(step):
         if step == 0:
-            load.wait()
+            out_load.wait()
         for dz, dy in OTHERS:
-            done = dy == 0 and dz > 0 if SPREAD_Z_FIRST[step] else (dz, dy) == (0, 1)
+            if SPREAD_Z_FIRST[step]:
+                done = dy == 0
+            else:
+                done = dz == 4 - relay(step) or (dz, dy) == (0, 1)
             if not done:
                 pl.when(place.active(dz))(functools.partial(receive, step, dz, dy))
 
@@ -465,7 +532,7 @@
 
         lax.fori_loop(0, 6, mine, 0)
 
-    def stage_d(step):
+    def stage_e(step):
         dx, dyh = DEPART[step]
         traffic.arrive(cr.at[step], c_s.at[step], c_r.at[step])
         way = {1: 0, 3: 1}.get(dx)
@@ -512,10 +579,15 @@
         elif dyh == 1:
             traffic.send(lambda: (pb.at[0, 1], yr, y_s, y_r, place.device(dyh=1)))
 
-    for turn in range(11):
-        for lag, stage in enumerate((stage_a, stage_b, stage_c, stage_d)):
-            if 0 <= turn - lag < 8:
-                stage(turn - lag)
+    schedule(ATTEND_LAGS, (stage_a, stage_b, stage_c, stage_d, stage_e))
+
+
+def block_kernel(act_ref, w_ref, wo_ref, out_ref, qkv, wov, *scratch):
+    place = Place()
+    traffic = Traffic(place)
+    cut = len(PROJECT_SCRATCH)
+    out_load = project(place, traffic, act_ref, w_ref, wo_ref, wov, qkv, *scratch[:cut])
+    attend_all(place, traffic, out_load, qkv, out_ref, wov, *scratch[cut:])
     traffic.drain()
 
 
@@ -523,60 +595,56 @@
     return pltpu.SemaphoreType.DMA(shape) if shape else pltpu.SemaphoreType.DMA
 
 
-def project(activations, weight):
+PROJECT_SCRATCH = (
+    pltpu.VMEM((3, 1536, 768), BF16),
+    pltpu.VMEM((4, 2, 2, 128, 1536), BF16),
+    pltpu.VMEM((8, 4, 2, 256, 384), BF16),
+    pltpu.VMEM((8, ZY[1], 384), BF16),
+    pltpu.VMEM((8, 4, YZ[1], 384), BF16),
+    pltpu.VMEM((8, 2, 2, ZY[2], 384), BF16),
+    pltpu.VMEM((8, 2, YZ[2], 384), BF16),
+    pltpu.VMEM((8, 2, 2, ZY[1], 384), BF16),
+    pltpu.VMEM((8, 2, YZ[1], 384), BF16),
+    pltpu.VMEM((8, 8, 128), F32),
+    dma(4), dma(8), dma(8), dma(16), dma(4, 2, 2), dma(8), dma(8), dma(8, 4), dma(8, 4),
+    dma(2, 8, 2), dma(2, 8, 2), dma(2, 8, 2), dma(2, 8, 2),
+)
+ATTEND_SCRATCH = (
+    pltpu.VMEM((8, 256, 768), BF16),
+    pltpu.VMEM((256, 2048), F32),
+    pltpu.VMEM((2, 128, 1536), F32),
+    pltpu.VMEM((8, 128, 1536), BF16),
+    pltpu.VMEM((8, 128, 1536), BF16),
+    pltpu.VMEM((4, 2, 128, 1536), BF16),
+    pltpu.VMEM((2, 2, 64, 1536), BF16),
+    pltpu.VMEM((2, 2, 128, 1536), BF16),
+    pltpu.VMEM((128, 1536), BF16),
+    dma(8, 8), dma(8, 4, 2), dma(8), dma(8),
+    dma(2, 2), dma(2, 2), dma(2, 2), dma(2, 2), dma(), dma(),
+)
+
+
+def per_device(activations, qkv_weight, out_weight):
     return pl.pallas_call(
-        project_kernel,
-        out_shape=jax.ShapeDtypeStruct((2048, 384), BF16),
-        in_specs=[pl.BlockSpec(memory_space=pltpu.VMEM), pl.BlockSpec(memory_space=pl.ANY)],
+        block_kernel,
+        out_shape=jax.ShapeDtypeStruct((128, 1536), BF16),
+        in_specs=[
+            pl.BlockSpec(memory_space=pltpu.VMEM),
+            pl.BlockSpec(memory_space=pl.ANY),
+            pl.BlockSpec(memory_space=pl.ANY),
+        ],
         out_specs=pl.BlockSpec(memory_space=pltpu.VMEM),
         scratch_shapes=[
-            pltpu.VMEM((3, 1536, 768), BF16),
-            pltpu.VMEM((4, 2, 2, 128, 1536), BF16),
-            pltpu.VMEM((8, 4, 2, 256, 384), BF16),
-            pltpu.VMEM((8, 4, 256, 384), BF16),
-            pltpu.VMEM((8, 2, 2, 128, 384), BF16),
-            pltpu.VMEM((8, 2, 2, 256, 384), BF16),
-            pltpu.VMEM((8, 8, 128), F32),
-            dma(3), dma(8), dma(8), dma(16), dma(4, 2, 2), dma(8, 4), dma(8, 4),
-            dma(8, 2), dma(8, 2), dma(8, 2), dma(8, 2),
+            pltpu.VMEM((2048, 384), BF16),
+            pltpu.VMEM((768, 1536), BF16),
+            *PROJECT_SCRATCH,
+            *ATTEND_SCRATCH,
         ],
         compiler_params=pltpu.CompilerParams(
-            collective_id=1, has_side_effects=True, vmem_limit_bytes=56 << 20
+            collective_id=1, has_side_effects=True, vmem_limit_bytes=60 << 20
         ),
-        name="project",
-    )(activations, weight)
-
-
-def attend(qkv, weight):
-    return pl.pallas_call(
-        attend_kernel,
-        out_shape=jax.ShapeDtypeStruct((128, 1536), BF16),
-        in_specs=[pl.BlockSpec(memory_space=pltpu.VMEM), pl.BlockSpec(memory_space=pl.ANY)],
-        out_specs=pl.BlockSpec(memory_space=pltpu.VMEM),
-        scratch_shapes=[
-            pltpu.VMEM((768, 1536), BF16),
-            pltpu.VMEM((8, 256, 768), BF16),
-            pltpu.VMEM((256, 2048), F32),
-            pltpu.VMEM((2, 128, 1536), F32),
-            pltpu.VMEM((8, 128, 1536), BF16),
-            pltpu.VMEM((8, 128, 1536), BF16),
-            pltpu.VMEM((4, 2, 128, 1536), BF16),
-            pltpu.VMEM((2, 2, 64, 1536), BF16),
-            pltpu.VMEM((2, 2, 128, 1536), BF16),
-            pltpu.VMEM((128, 1536), BF16),
-            dma(), dma(8, 8), dma(8, 4, 2), dma(8), dma(8),
-            dma(2, 2), dma(2, 2), dma(2, 2), dma(2, 2), dma(), dma(),
-        ],
-        compiler_params=pltpu.CompilerParams(
-            collective_id=2, has_side_effects=True, vmem_limit_bytes=56 << 20
-        ),
-        name="attend",
-    )(qkv, weight)
-
-
-def per_device(activations, qkv_weight, out_weight):
-    qkv = project(activations, jnp.transpose(qkv_weight, (1, 0, 2)))
-    return attend(qkv, out_weight)
+        name="block",
+    )(activations, jnp.transpose(qkv_weight, (1, 0, 2)), out_weight)
 
 
 def solution(mesh):

time: 181 us -> 158 us (0.87)
  Pallas kernels: 179 us -> 156 us
    pallas_call x2 -> x1, Pallas kernels: 179 us -> 156 us  [per_device(): pl.pallas_call(block_kernel, out_shape=jax.ShapeDtypeStruct((128, 1536),...]
where the time goes in v2:
time: 158 us
  Pallas kernels  156 us (99%)
  local copies, waits for them, and re-layouts  1.77 us (1%)
    pallas_call x1, Pallas kernels, per_device(): pl.pallas_call(block_kernel, out_shape=jax.ShapeDtypeStruct((128, 1536),...  156 us

profile of v2, /device:TPU:4, one launch (start us, length us, event | category | flops | bytes accessed | tf_op | source)
XLA Modules:
  0.0 157.7 jit_solution(9747704284056142219)
XLA Ops:
  0.0 155.9 %block.1 = bf16[128,1536]{1,0:T(8,128)(2,1)} custom-call(bf16[128,1536]{1,0:T(8,128)(2,1)} %act_ref.1, bf16[3,1536,768]{2,1,0:T(8,128)(2,1)} %bitcast.1, bf16[768,1536]{1,0:T(8,128)(2,1)} %wo_ref.1), custom_call_target="tpu_custom_call" | custom-call | tf_op jit(solution)/shard_map/block/pallas_call | solution.py:628
  155.9 1.8 %copy.5 = bf16[128,1536]{1,0:T(8,128)(2,1)} copy(bf16[128,1536]{1,0:T(8,128)(2,1)} %block.1) | data formatting | bytes 786432

commit v3 on v2

--- a/solution.py
+++ b/solution.py
@@ -203,19 +203,17 @@
     def stage_project(step):
         dx, dyh = ARRIVAL[step]
 
-        def tile(i, carry):
-            kind, level = i // 3, i % 3
-            columns = pl.ds(pl.multiple_of(level * 256, 256), 256)
+        def tile(kind, carry):
             part = jnp.dot(
-                nb[dx, dyh].reshape(256, 1536), wv[kind, :, columns], preferred_element_type=F32
+                nb[dx, dyh].reshape(256, 1536), wv[kind], preferred_element_type=F32
             ).astype(BF16)
-            dz = (level + 8 - 2 * core - z) % 4
             where = pl.ds(pl.multiple_of(kind * 128, 128), 128)
-            for side in range(2):
-                pb[step, dz, (side + y) % 2, :, where] = part[:, side * 128 : side * 128 + 128]
+            for head in range(6):
+                dz = (head // 2 + 8 - 2 * core - z) % 4
+                pb[step, dz, (head + y) % 2, :, where] = part[:, head * 128 : head * 128 + 128]
             return carry
 
-        lax.fori_loop(0, 9, tile, 0)
+        lax.fori_loop(0, 3, tile, 0)
 
     def rows_of(part, way):
         low, count, first = part
@@ -237,6 +235,29 @@
                 2,
             )
 
+    def near(part, step, way, half):
+        rows = rows_of(part, half)
+        into = pl.ds(rows.start - part[0], rows.size)
+        return rows, zbz.at[step, way, :, into] if part is ZY else zby.at[step, way, into]
+
+    def send_near(part, step, way, half):
+        both, hop = part is ZY, 1 + 2 * way
+
+        def build():
+            rows, into = near(part, step, way, half)
+            return (
+                pb.at[step, hop, :, rows] if both else pb.at[step, hop, 0, rows],
+                into,
+                b_s.at[int(both), step, way, half],
+                b_r.at[int(both), step, way, half],
+                place.device(dz=hop),
+            )
+
+        traffic.send(build, hop)
+
+    def z_alone(part, step, way):
+        pl.when(place.active(1 + 2 * way))(lambda: send_near(part, step, way, 1 - way))
+
     def z_near(part, step):
         both = part is ZY
         for way, hop in ((0, 1), (1, 3)):
@@ -252,35 +273,26 @@
                 for side in range(2 if both else 1):
 
                     def add(tile, side=side):
-                        here = pl.ds(pl.multiple_of(tile.start + rows.start, 16), 16)
+                        here = pl.ds(pl.multiple_of(tile.start + rows.start, 16), tile.size)
                         far = caz[step, way, side, tile, :] if both else cay[step, way, tile, :]
                         pb[step, hop, side, here, :] = (
                             pb[step, hop, side, here, :].astype(F32) + far.astype(F32)
                         ).astype(BF16)
 
-                    row_tiles(rows.size, 16, add)
-                whole = pl.ds(part[0], part[1])
-                traffic.send(
-                    lambda: (
-                        pb.at[step, hop, :, whole] if both else pb.at[step, hop, 0, whole],
-                        zbz.at[step, way] if both else zby.at[step, way],
-                        b_s.at[int(both), step, way],
-                        b_r.at[int(both), step, way],
-                        place.device(dz=hop),
-                    ),
-                    hop,
-                )
+                    row_tiles(rows.size, 64, add)
+                send_near(part, step, way, way)
 
             pl.when(place.active(hop))(go)
 
     def arrive_near(part, step):
         both = part is ZY
         for way in range(2):
-            traffic.arrive(
-                zbz.at[step, way] if both else zby.at[step, way],
-                b_s.at[int(both), step, way],
-                b_r.at[int(both), step, way],
-            )
+            for half in range(2):
+                traffic.arrive(
+                    near(part, step, way, half)[1],
+                    b_s.at[int(both), step, way, half],
+                    b_r.at[int(both), step, way, half],
+                )
 
     def send_y(step, dz):
         traffic.send(
@@ -300,6 +312,8 @@
         pl.when(place.active(2))(functools.partial(z_far, ZY, step))
         for dz in (2, 1, 3, 0):
             pl.when(place.active(dz))(functools.partial(send_y, step, dz))
+        for way in range(2):
+            z_alone(ZY, step, way)
 
     def stage_b(step):
         z_near(ZY, step)
@@ -309,16 +323,18 @@
                 traffic.arrive(yry.at[step, dz], y_s.at[step, dz], y_r.at[step, dz])
 
                 def add(tile):
-                    here = pl.ds(pl.multiple_of(tile.start + YZ[0], 16), 16)
+                    here = pl.ds(pl.multiple_of(tile.start + YZ[0], 16), tile.size)
                     pb[step, dz, 0, here, :] = (
                         pb[step, dz, 0, here, :].astype(F32) + yry[step, dz, tile, :].astype(F32)
                     ).astype(BF16)
 
-                row_tiles(YZ[1], 16, add)
+                row_tiles(YZ[1], 64, add)
                 if dz == 2:
                     z_far(YZ, step)
 
             pl.when(place.active(dz))(go)
+            if dz != 2:
+                z_alone(YZ, step, dz // 2)
 
     def stage_c(step):
         z_near(YZ, step)
@@ -333,7 +349,7 @@
                     + zbz[step, 1, 1, tile, :].astype(F32)
                 ).astype(BF16)
 
-            row_tiles(ZY[1], 16, add)
+            row_tiles(ZY[1], 64, add)
             traffic.send(
                 lambda: (
                     pb.at[step, 0, 1, pl.ds(ZY[0], ZY[1])], yrz.at[step], yz_s.at[step],
@@ -354,8 +370,8 @@
 
             def finish(low, yr, zb0, zb1):
                 def add(tile):
-                    mine = pl.ds(pl.multiple_of(tile.start + low, 16), 16)
-                    here = pl.ds(pl.multiple_of(tile.start + low + t * 256, 16), 16)
+                    mine = pl.ds(pl.multiple_of(tile.start + low, 16), tile.size)
+                    here = pl.ds(pl.multiple_of(tile.start + low + t * 256, 16), tile.size)
                     qkv[here, :] = (
                         pb[step, 0, 0, mine, :].astype(F32)
                         + yr[tile, :].astype(F32)
@@ -366,10 +382,10 @@
                 return add
 
             row_tiles(
-                ZY[1], 16, finish(ZY[0], yrz.at[step], zbz.at[step, 0, 0], zbz.at[step, 1, 0])
+                ZY[1], 64, finish(ZY[0], yrz.at[step], zbz.at[step, 0, 0], zbz.at[step, 1, 0])
             )
             row_tiles(
-                YZ[1], 16, finish(YZ[0], yry.at[step, 0], zby.at[step, 0], zby.at[step, 1])
+                YZ[1], 64, finish(YZ[0], yry.at[step, 0], zby.at[step, 0], zby.at[step, 1])
             )
 
         pl.when(place.active(0))(go)
@@ -394,10 +410,11 @@
 
     def attend(step):
         t = place.chunk(*DEPART[step])
+        last = t // 2
         query = qkv_ref[pl.ds(pl.multiple_of(t * 256, 256), 256), 0:128]
 
         def block(j):
-            return pl.ds(pl.multiple_of(j * 256, 256), 256)
+            return pl.ds(pl.multiple_of(j * 512, 512), 512)
 
         def scores(j):
             return lax.dot_general(
@@ -405,29 +422,32 @@
                 preferred_element_type=F32,
             )
 
+        def fold(op, wide):
+            return op(op(wide[:, :128], wide[:, 128:256]), op(wide[:, 256:384], wide[:, 384:]))
+
         def first(j, top):
             now = scores(j)
             score[:, block(j)] = now
-            return jnp.maximum(top, jnp.maximum(now[:, :128], now[:, 128:]))
-
-        row = lax.broadcasted_iota(jnp.int32, (256, 256), 0)
-        col = lax.broadcasted_iota(jnp.int32, (256, 256), 1)
-        now = jnp.where(row >= col, scores(t), F32(-1e30))
-        score[:, block(t)] = now
-        top = lax.fori_loop(0, t, first, jnp.maximum(now[:, :128], now[:, 128:]))
+            return jnp.maximum(top, fold(jnp.maximum, now))
+
+        row = lax.broadcasted_iota(jnp.int32, (256, 512), 0)
+        col = lax.broadcasted_iota(jnp.int32, (256, 512), 1)
+        now = jnp.where(row + (t % 2) * 256 >= col, scores(last), F32(-1e30))
+        score[:, block(last)] = now
+        top = lax.fori_loop(0, last, first, fold(jnp.maximum, now))
         top = jnp.max(top, 1, keepdims=True)
 
         def second(j, state):
             low, mixed = state
             weight = jnp.exp2((score[:, block(j)] - top) * factor)
-            low = low + (weight[:, :128] + weight[:, 128:])
+            low = low + fold(jnp.add, weight)
             mixed = mixed + jnp.dot(
                 weight.astype(BF16), qkv_ref[block(j), 256:384], preferred_element_type=F32
             )
             return low, mixed
 
         zero = jnp.zeros((256, 128), F32)
-        low, mixed = lax.fori_loop(0, t + 1, second, (zero, zero))
+        low, mixed = lax.fori_loop(0, last + 1, second, (zero, zero))
         at[step, :, head_columns(0, 0)] = (mixed / jnp.sum(low, 1, keepdims=True)).astype(BF16)
 
     spread = []
@@ -509,28 +529,19 @@
                 pl.when(place.active(dz))(functools.partial(receive, step, dz, dy))
 
         def half(which):
-            return at[step, pl.ds(pl.multiple_of(which * 128, 128), 128), :]
-
-        def theirs(i, carry):
-            columns = pl.ds(pl.multiple_of(i * 256, 256), 256)
-            cs[step, :, columns] = jnp.dot(
-                half(1 - core), wv[:, columns], preferred_element_type=F32
-            ).astype(BF16)
+            return pl.ds(pl.multiple_of(which * 128, 128), 128)
+
+        def tile(i, carry):
+            columns = pl.ds(pl.multiple_of(i * 512, 512), 512)
+            score[:, 0:512] = jnp.dot(at[step], wv[:, columns], preferred_element_type=F32)
+            cs[step, :, columns] = score[half(1 - core), 0:512].astype(BF16)
+            acc[step % 2, :, columns] = score[half(core), 0:512]
             return carry
 
-        lax.fori_loop(0, 6, theirs, 0)
+        lax.fori_loop(0, 3, tile, 0)
         traffic.send(
             lambda: (cs.at[step], cr.at[step], c_s.at[step], c_r.at[step], place.device(dcore=1))
         )
-
-        def mine(i, carry):
-            columns = pl.ds(pl.multiple_of(i * 256, 256), 256)
-            acc[step % 2, :, columns] = jnp.dot(
-                half(core), wv[:, columns], preferred_element_type=F32
-            )
-            return carry
-
-        lax.fori_loop(0, 6, mine, 0)
 
     def stage_e(step):
         dx, dyh = DEPART[step]
@@ -546,7 +557,7 @@
 
         def combine(lo):
             def add(rows):
-                here = pl.ds(pl.multiple_of(rows.start + lo * 64, 16), 16)
+                here = pl.ds(pl.multiple_of(rows.start + lo * 64, 16), rows.size)
                 now = acc[step % 2, here, :] + cr[step, here, :].astype(F32)
                 if way is not None and lo == way:
                     now = now + ca[dyh, way, rows, :].astype(F32)
@@ -557,7 +568,7 @@
                 else:
                     pb[dx, dyh, here, :] = now.astype(BF16)
 
-            row_tiles(64, 16, add)
+            row_tiles(64, 32, add)
 
         combine(0)
         combine(1)
@@ -607,7 +618,7 @@
     pltpu.VMEM((8, 2, YZ[1], 384), BF16),
     pltpu.VMEM((8, 8, 128), F32),
     dma(4), dma(8), dma(8), dma(16), dma(4, 2, 2), dma(8), dma(8), dma(8, 4), dma(8, 4),
-    dma(2, 8, 2), dma(2, 8, 2), dma(2, 8, 2), dma(2, 8, 2),
+    dma(2, 8, 2), dma(2, 8, 2), dma(2, 8, 2, 2), dma(2, 8, 2, 2),
 )
 ATTEND_SCRATCH = (
     pltpu.VMEM((8, 256, 768), BF16),

time: 158 us -> 147 us (0.930)
  Pallas kernels: 156 us -> 145 us
    pallas_call x1, Pallas kernels: 156 us -> 145 us  [per_device(): pl.pallas_call(block_kernel, out_shape=jax.ShapeDtypeStruct((128, 1536),...]
where the time goes in v3:
time: 147 us
  Pallas kernels  145 us (99%)
  local copies, waits for them, and re-layouts  1.77 us (1%)
    pallas_call x1, Pallas kernels, per_device(): pl.pallas_call(block_kernel, out_shape=jax.ShapeDtypeStruct((128, 1536),...  145 us

profile of v3, /device:TPU:4, one launch (start us, length us, event | category | flops | bytes accessed | tf_op | source)
XLA Modules:
  0.0 147.3 jit_solution(12834326865682621201)
XLA Ops:
  0.0 145.5 %block.1 = bf16[128,1536]{1,0:T(8,128)(2,1)} custom-call(bf16[128,1536]{1,0:T(8,128)(2,1)} %act_ref.1, bf16[3,1536,768]{2,1,0:T(8,128)(2,1)} %bitcast.1, bf16[768,1536]{1,0:T(8,128)(2,1)} %wo_ref.1), custom_call_target="tpu_custom_call" | custom-call | tf_op jit(solution)/shard_map/block/pallas_call | solution.py:639
  145.5 1.8 %copy.5 = bf16[128,1536]{1,0:T(8,128)(2,1)} copy(bf16[128,1536]{1,0:T(8,128)(2,1)} %block.1) | data formatting | bytes 786432

commit v4 on v3

--- a/solution.py
+++ b/solution.py
@@ -15,7 +15,7 @@
 BF16 = jnp.bfloat16
 
 ARRIVAL = ((0, 0), (0, 1), (1, 0), (3, 0), (2, 0), (1, 1), (3, 1), (2, 1))
-PROJECT_LAGS = (0, 1, 2, 3)
+PROJECT_LAGS = (0, 1, 2, 4)
 ATTEND_LAGS = (0, 1, 2, 3, 4)
 ZY = (0, 128, 64)
 YZ = (128, 128, 64)

time: 147 us -> 150 us (1.020); the launches traced: 147 us -> 148 us
  no operation moved by 1% of the time
where the time goes in v4:
time: 150 us; the launch traced here: 148 us
  Pallas kernels  146 us (97%)
  local copies, waits for them, and re-layouts  1.77 us (1%)
    pallas_call x1, Pallas kernels, per_device(): pl.pallas_call(block_kernel, out_shape=jax.ShapeDtypeStruct((128, 1536),...  146 us

profile of v4, /device:TPU:4, one launch (start us, length us, event | category | flops | bytes accessed | tf_op | source)
XLA Modules:
  0.0 147.6 jit_solution(14189612721760459438)
XLA Ops:
  0.0 145.9 %block.1 = bf16[128,1536]{1,0:T(8,128)(2,1)} custom-call(bf16[128,1536]{1,0:T(8,128)(2,1)} %act_ref.1, bf16[3,1536,768]{2,1,0:T(8,128)(2,1)} %bitcast.1, bf16[768,1536]{1,0:T(8,128)(2,1)} %wo_ref.1), custom_call_target="tpu_custom_call" | custom-call | tf_op jit(solution)/shard_map/block/pallas_call | solution.py:639
  145.9 1.8 %copy.5 = bf16[128,1536]{1,0:T(8,128)(2,1)} copy(bf16[128,1536]{1,0:T(8,128)(2,1)} %block.1) | data formatting | bytes 786432
